TPU v7x, 256 devices: a whole 4x4x8 slice. The times are simulated.
256 devices in a mesh: replica: 32 (over y, z), fsdp: 8 (over x, core).
Axes of the slice: x: 4, y: 4, z: 8, core: 2. Of those that a mesh axis runs over, the one named last changes fastest.
Arguments:
- outer_param: float32 [512, 8192], P('fsdp'), may hold values from -4 to 4
- momentum: float32 [512, 8192], P('fsdp'), may hold values from -3 to 3
- inner_weights: bfloat16 [32, 512, 8192], P('replica', 'fsdp'), may hold values from -80 to 80
Outputs:
- new_outer: float32 [512, 8192], P('fsdp')
- new_momentum: float32 [512, 8192], P('fsdp')
- merged: bfloat16 [32, 512, 8192], P('replica', 'fsdp')
All inputs are finite; a program needn't handle non-finite values.
Results may differ from a plain program's by a relative error of at most 0.001.
Values sent between devices are 32-bit elements; how exact they have to be, the bound alone decides.
A program may use at most 64 MiB of HBM per device.

v0:
```python
import jax
import jax.numpy as jnp
from jax import lax
from jax.sharding import PartitionSpec as P


def outer_update(share, factor, momentum, outer_param):
    grad = factor * share
    new_momentum = 0.9 * momentum + grad
    new_outer = outer_param - 0.7 * (grad + 0.9 * new_momentum)
    return (new_outer, new_momentum)


def clip_factor(squares, entries):
    return jnp.minimum(1.0, 0.5 / jnp.sqrt(squares / entries + 1e-06))


def body(outer_param, momentum, inner_weights):
    local = outer_param - inner_weights[0].astype(jnp.float32)
    count = lax.axis_size("replica")
    entries = outer_param.shape[0] * lax.axis_size("fsdp") * outer_param.shape[1]
    pseudo = lax.psum(local, "replica") / count
    squares = lax.psum(jnp.sum(pseudo * pseudo), "fsdp")
    new_outer, new_momentum = outer_update(
        pseudo, clip_factor(squares, entries), momentum, outer_param
    )
    merged = (0.5 * inner_weights.astype(jnp.float32) + 0.5 * new_outer[None]).astype(jnp.bfloat16)
    return (new_outer, new_momentum, merged)


def solution(mesh):
    in_specs = (P("fsdp", None), P("fsdp", None), P("replica", "fsdp", None))
    out_specs = (P("fsdp", None), P("fsdp", None), P("replica", "fsdp", None))
    return jax.shard_map(body, mesh=mesh, in_specs=in_specs, out_specs=out_specs, check_vma=False)
```

profile of v0, /device:TPU:2, one launch (start us, length us, event | category | flops | bytes accessed | tf_op | source)
XLA Modules:
  0.0 195.6 jit_solution(7122107078134407097)
XLA Ops:
  7.2 0.0 all-reduce.2.cloned.1.call-start
  7.2 3.4 %fusion = f32[64,8192]{1,0:T(8,128)} fusion(f32[64,8192]{1,0:T(8,128)} %param.3, bf16[1,64,8192]{2,1,0:T(8,128)(2,1)} %param.5), kind=kLoop, calls=%fused_computation.2 | loop fusion | flops 1048576 | bytes 5242880 | tf_op jit(solution)/shard_map/sub | solution.py:19
  10.6 0.0 copy-start
  10.6 0.0 copy-start.1
  10.6 0.0 all-reduce.2.cloned.1.call-update
  10.6 158.9 %all-reduce.2.cloned.1.call-done = f32[64,8192]{1,0:T(8,128)} async-done(((f32[64,8192]{1,0:T(8,128)}), f32[64,8192]{1,0:T(8,128)}) %all-reduce.2.cloned.1.call-update) | async-done | bytes 2097168 | tf_op jit(solution)/shard_map/psum | solution.py:22
  169.5 2.7 %multiply_reduce_fusion = f32[]{:T(128)} fusion(f32[64,8192]{1,0:T(8,128)} %all-reduce.2.cloned.1.call-done), kind=kLoop, calls=%fused_computation.7 | loop fusion | flops 1572863 | bytes 2097156 | tf_op jit(solution)/shard_map/reduce_sum | solution.py:23
  172.2 10.6 %psum.15 = f32[]{:T(128)} all-reduce(f32[]{:T(128)} %multiply_reduce_fusion), channel_id=1, replica_groups=mesh['replica'=32,'fsdp'=8] {'fsdp'}, use_global_device_ids=true, to_apply=%region_2.0 | all-reduce | flops 1 | bytes 8 | tf_op jit(solution)/shard_map/psum | solution.py:23
  183.5 0.0 copy-done
  183.5 0.0 copy-done.1
  183.5 5.2 %fusion.2 = (bf16[1,64,8192]{2,1,0:T(8,128)(2,1)}, f32[64,8192]{1,0:T(8,128)}, f32[64,8192]{1,0:T(8,128)}) fusion(bf16[1,64,8192]{2,1,0:T(8,128)(2,1)S(1)} %copy-done.1, f32[64,8192]{1,0:T(8,128)S(1)} %copy-done, f32[64,8192]{1,0:T(8,128)} %all-reduce.2.cloned.1.call-done, f32[]{:T(128)S(6)} %mul.28, f32[64,8192]{1,0:T(8,128)} %param.4), kind=kLoop, calls=%fused_computation.4 | loop fusion | flops 5767168 | bytes 12582916 | tf_op jit(solution)/shard_map/convert_element_type | solution.py:27
Async XLA Ops:
  7.2 162.3 %all-reduce.2.cloned.1.call-start = ((), (), s32[]{:S(2)}) async-start(), calls=%async_computation | async-start | bytes 4194304 | tf_op jit(solution)/shard_map/psum | solution.py:22
  10.6 173.0 %copy-start = (f32[64,8192]{1,0:T(8,128)S(1)}, f32[64,8192]{1,0:T(8,128)}, u32[]{:S(2)}) copy-start(f32[64,8192]{1,0:T(8,128)} %param.3) | copy-start | bytes 6291460
  10.6 173.0 %copy-start.1 = (bf16[1,64,8192]{2,1,0:T(8,128)(2,1)S(1)}, bf16[1,64,8192]{2,1,0:T(8,128)(2,1)}, u32[]{:S(2)}) copy-start(bf16[1,64,8192]{2,1,0:T(8,128)(2,1)} %param.5) | copy-start | bytes 3145732
Sparse Core Ops, SparseCore 0:
  12.1 157.3 all-reduce.1
where the time goes:
time: 199 us; the launch traced here: 196 us
  waiting for transfers between devices  159 us (80%)
  between operations  14.7 us (7%)
  other arithmetic  11.3 us (6%)
  blocking collectives  10.6 us (5%)
    psum x1, waiting for transfers between devices, body(): pseudo = lax.psum(local, 'replica') / count  159 us
    psum x1, blocking collectives, body(): squares = lax.psum(jnp.sum(pseudo * pseudo), 'fsdp')  10.6 us
    convert_element_type x1, other arithmetic, body(): (0.5 * inner_weights.astype(jnp.float32) + 0.5 * new_outer[None]).astype(...  5.21 us
  transfers between devices with their start and end apart: 1, of which 1 were waited for; matrix products, arithmetic and copies ran while one was open for 0% of the time, Pallas kernels for 0%

commit v1 on v0

v1 whole, which is shorter than its diff:
```python
import jax
import jax.numpy as jnp
from jax import lax
from jax.experimental import pallas as pl
from jax.experimental.pallas import tpu as pltpu
from jax.sharding import PartitionSpec as P

MESH = pl.DeviceIdType.MESH
NY, NZ, NF = 4, 8, 8
ROWS, COLS = 64, 8192
REPLICAS = 32
ENTRIES = 512 * 8192
FLOWS = (
    ("zy", 0, 3072, 3, 1),
    ("yz", 3072, 5120, 2, 2),
)
MAX_COPIES = 128
FROM_Z = {1: 0, -1: 1, 2: 2, -2: 3}
FROM_Y = {1: 4, -1: 5, 2: 6}
PLANES = 7
PEERS = (
    [(0, d, 0, 0) for d in range(1, NZ)] + [(d, 0, 0, 0) for d in range(1, NY)] + [(0, 0, d, 0) for d in range(1, 4)] + [(0, 0, 0, 1)]
)


class AllReduce:
    def __init__(self, acc, got, full, send_sems, recv_sems):
        self.acc, self.got, self.full = acc, got, full
        self.send_sems, self.recv_sems = send_sems, recv_sems
        r, f = lax.axis_index("replica"), lax.axis_index("fsdp")
        self.y, self.z = r // NZ, r % NZ
        self.x, self.c = f // 2, f % 2
        self.sent = []
        self.squares = []

    def device(self, dy=0, dz=0, dx=0, dc=0):
        y, z, x, c = self.y, self.z, self.x, self.c
        y = lax.rem(y + (dy % NY), NY) if dy else y
        z = lax.rem(z + (dz % NZ), NZ) if dz else z
        x = lax.rem(x + (dx % 4), 4) if dx else x
        c = 1 - c if dc else c
        return (y * NZ + z, x * 2 + c)

    def copy(self, src, dst, to):
        i = len(self.sent)
        assert i < MAX_COPIES
        c = pltpu.make_async_remote_copy(
            src_ref=src, dst_ref=dst, send_sem=self.send_sems.at[i], recv_sem=self.recv_sems.at[i],
            device_id=to, device_id_type=MESH)
        c.start()
        self.sent.append(c)
        return c

    @staticmethod
    def at(region):
        r, n, c, w = region
        return (pl.ds(r, n), pl.ds(c, w))

    def push(self, region, to, plane):
        rs, cs = self.at(region)
        return self.copy(self.acc.at[rs, cs], self.got.at[plane, rs, cs], to)

    def pass_on(self, region, to):
        rs, cs = self.at(region)
        return self.copy(self.full.at[rs, cs], self.full.at[rs, cs], to)

    def add(self, region, planes):
        rs, cs = self.at(region)
        total = self.acc[rs, cs]
        for p in planes:
            total = total + self.got[p, rs, cs]
        self.acc[rs, cs] = total

    def shard(self, d, c, w):
        g = lax.rem(self.z + (d % NZ), NZ) if d % NZ else self.z
        return (pl.multiple_of(g * 8, 8), 8, c, w)

    def half_shard(self, d, c, w, s):
        h = w // 2
        return self.shard(d, c if s > 0 else c + h, h)

    def scatter_z(self, c, w, depth):
        sh = lambda d: self.shard(d, c, w)
        z = lambda d: self.device(dz=d)
        both = (1, -1)
        if depth == 4:
            m = {s: self.push(self.half_shard(4, c, w, s), z(s), FROM_Z[s]) for s in both}
            yield
            for s in both:
                m[s].wait_recv()
                self.add(self.half_shard(3 * s, c, w, s), [FROM_Z[s]])
                m[s] = self.push(sh(3 * s), z(s), FROM_Z[s])
            yield
            for s in both:
                m[s].wait_recv()
                self.add(sh(2 * s), [FROM_Z[s]])
                m[s] = self.push(sh(2 * s), z(s), FROM_Z[s])
            yield
        else:
            far = {s: self.push(self.half_shard(4, c, w, s), z(2 * s), FROM_Z[2 * s]) for s in both}
            m = {s: self.push(sh(3 * s), z(s), FROM_Z[s]) for s in both}
            if depth == 2:
                near = {s: self.push(sh(s), z(s), FROM_Z[s]) for s in both}
            yield
            for s in both:
                m[s].wait_recv()
                self.add(sh(2 * s), [FROM_Z[s]])
                far[s].wait_recv()
                self.add(self.half_shard(2 * s, c, w, s), [FROM_Z[2 * s]])
                if depth == 3:
                    m[s] = self.push(sh(2 * s), z(s), FROM_Z[s])
                else:
                    far[s] = self.push(sh(2 * s), z(2 * s), FROM_Z[2 * s])
            yield
            if depth == 2:
                for s in both:
                    near[s].wait_recv()
                    far[s].wait_recv()
                self.add(sh(0), [FROM_Z[d] for d in (1, -1, 2, -2)])
                return
        for s in both:
            m[s].wait_recv()
            self.add(sh(s), [FROM_Z[s]])
            m[s] = self.push(sh(s), z(s), FROM_Z[s])
        yield
        for s in both:
            m[s].wait_recv()
        self.add(sh(0), [FROM_Z[1], FROM_Z[-1]])

    def gather_z(self, c, w, depth):
        sh = lambda d: self.shard(d, c, w)
        z = lambda d: self.device(dz=d)
        both = (1, -1)
        if depth == 2:
            far = {s: self.pass_on(sh(0), z(2 * s)) for s in both}
            near = {s: self.pass_on(sh(0), z(s)) for s in both}
            yield
            for s in both:
                far[s].wait_recv()
                far[s] = self.pass_on(self.half_shard(-2 * s, c, w, s), z(2 * s))
                near[s, 2] = self.pass_on(sh(-2 * s), z(s))
            yield
            for m in (near, far):
                for v in m.values():
                    v.wait_recv()
            return
        m = {s: self.pass_on(sh(0), z(s)) for s in both}
        yield
        for s in both:
            m[s].wait_recv()
            m[s] = self.pass_on(sh(-s), z(s))
        yield
        far = {}
        for s in both:
            m[s].wait_recv()
            if depth == 3:
                far[s] = self.pass_on(self.half_shard(-2 * s, c, w, s), z(2 * s))
            m[s] = self.pass_on(sh(-2 * s), z(s))
        yield
        for s in both:
            m[s].wait_recv()
            if depth == 4:
                far[s] = self.pass_on(self.half_shard(-3 * s, c, w, s), z(s))
        if depth == 4:
            yield
        for s in both:
            far[s].wait_recv()

    def quarter(self, d, r, n, c, w):
        q = lax.rem(self.y + (d % NY), NY) if d % NY else self.y
        return (r, n, pl.multiple_of(c + q * (w // 4), 128), w // 4)

    def half_quarter(self, d, r, n, c, w, s):
        r, n, c, w = self.quarter(d, r, n, c, w)
        if n > 8:
            return (r if s > 0 else r + n // 2, n // 2, c, w)
        return (r, n, c if s > 0 else pl.multiple_of(c + w // 2, 128), w // 2)

    def scatter_y(self, r, n, c, w, depth):
        part = lambda d: self.quarter(d, r, n, c, w)
        y = lambda d: self.device(dy=d)
        both = (1, -1)
        if depth == 1:
            ms = [self.push(part(d), y(d), FROM_Y[d]) for d in (2, 1, -1)]
            yield
            for m in ms:
                m.wait_recv()
            self.add(part(0), list(FROM_Y.values()))
            return
        m = {s: self.push(self.half_quarter(2, r, n, c, w, s), y(s), FROM_Y[s]) for s in both}
        yield
        for s in both:
            m[s].wait_recv()
            self.add(self.half_quarter(s, r, n, c, w, s), [FROM_Y[s]])
            m[s] = self.push(part(s), y(s), FROM_Y[s])
        yield
        for s in both:
            m[s].wait_recv()
        self.add(part(0), [FROM_Y[s] for s in both])

    def gather_y(self, r, n, c, w, depth):
        part = lambda d: self.quarter(d, r, n, c, w)
        y = lambda d: self.device(dy=d)
        both = (1, -1)
        if depth == 1:
            ms = [self.pass_on(part(0), y(d)) for d in (2, 1, -1)]
            yield
            for m in ms:
                m.wait_recv()
            return
        m = {s: self.pass_on(part(0), y(s)) for s in both}
        yield
        for s in both:
            m[s].wait_recv()
            m[s] = self.pass_on(self.half_quarter(-s, r, n, c, w, s), y(s))
        yield
        for s in both:
            m[s].wait_recv()

    def flow(self, order, c, w, z_depth, y_depth):
        mine = self.shard(0, *self.quarter(0, 0, 8, c, w)[2:])
        if order == "zy":
            yield from self.scatter_z(c, w, z_depth)
            yield from self.scatter_y(mine[0], 8, c, w, y_depth)
        else:
            yield from self.scatter_y(0, ROWS, c, w, y_depth)
            yield from self.scatter_z(mine[2], w // 4, z_depth)
        rs, cs = self.at(mine)
        pseudo = self.acc[rs, cs] / REPLICAS
        self.full[rs, cs] = pseudo
        self.squares.append(sum(pseudo[:, i:i + 128] * pseudo[:, i:i + 128] for i in range(0, w // 4, 128)))
        if order == "zy":
            yield from self.gather_y(mine[0], 8, c, w, y_depth)
            yield from self.gather_z(c, w, z_depth)
        else:
            yield from self.gather_z(mine[2], w // 4, z_depth)
            yield from self.gather_y(0, ROWS, c, w, y_depth)

    def clip(self, factor, sums, parts):
        while len(self.squares) < len(FLOWS):
            yield
        total = sum(self.squares)
        stages = [
            [dict(dc=1)], [dict(dx=d) for d in (2, 1, 3)], [dict(dy=d) for d in (2, 1, 3)], [dict(dz=d) for d in (4, 3, 5, 2, 6, 1, 7)]]
        n = 0
        for i, stage in enumerate(stages):
            sums[i] = total
            ms = [self.copy(sums.at[i], parts.at[n + j], self.device(**d)) for j, d in enumerate(stage)]
            yield
            for j, m in enumerate(ms):
                m.wait_recv()
                total = total + parts[n + j]
            n += len(stage)
        mean = jnp.full((8, 128), jnp.sum(total)) / ENTRIES
        factor[...] = jnp.minimum(1.0, 0.5 / jnp.sqrt(mean + 1e-6))


def kernel(outer_hbm, inner_hbm, full, factor, outer, inner, acc, got, sums, parts, send_sems, recv_sems, load_sems):
    ar = AllReduce(acc, got, full, send_sems, recv_sems)
    loads = []
    for i, (_, c, w, _, _) in enumerate(FLOWS):
        cs = pl.ds(c, w)
        for j, (src, dst) in enumerate(((outer_hbm, outer), (inner_hbm, inner))):
            loads.append(pltpu.make_async_copy(src.at[:, cs], dst.at[:, cs], load_sems.at[2 * i + j]))
            loads[-1].start()
    barrier = pltpu.get_barrier_semaphore()
    for p in PEERS:
        pl.semaphore_signal(barrier, inc=1, device_id=ar.device(*p), device_id_type=MESH)
    flows = []
    for i, (order, c, w, z_depth, y_depth) in enumerate(FLOWS):
        loads[2 * i].wait()
        loads[2 * i + 1].wait()
        acc[:, pl.ds(c, w)] = outer[:, pl.ds(c, w)] - inner[:, pl.ds(c, w)].astype(jnp.float32)
        if i == 0:
            pl.semaphore_wait(barrier, len(PEERS))
        g = ar.flow(order, c, w, z_depth, y_depth)
        next(g)
        flows.append(g)
    flows.append(ar.clip(factor, sums, parts))
    while flows:
        flows = [g for g in flows if next(g, flows) is None]
    for c in ar.sent:
        c.wait_send()


def all_reduce(outer_param, inner):
    n = 1 + 3 + 3 + 7
    return pl.pallas_call(
        kernel,
        out_shape=(jax.ShapeDtypeStruct((ROWS, COLS), jnp.float32), jax.ShapeDtypeStruct((8, 128), jnp.float32)),
        in_specs=[pl.BlockSpec(memory_space=pl.ANY)] * 2,
        out_specs=(pl.BlockSpec(memory_space=pltpu.VMEM),) * 2,
        scratch_shapes=[
            pltpu.VMEM((ROWS, COLS), jnp.float32),
            pltpu.VMEM((ROWS, COLS), jnp.bfloat16),
            pltpu.VMEM((ROWS, COLS), jnp.float32),
            pltpu.VMEM((PLANES, ROWS, COLS), jnp.float32),
            pltpu.VMEM((4, 8, 128), jnp.float32),
            pltpu.VMEM((n, 8, 128), jnp.float32),
            pltpu.SemaphoreType.DMA((MAX_COPIES,)),
            pltpu.SemaphoreType.DMA((MAX_COPIES,)),
            pltpu.SemaphoreType.DMA((2 * len(FLOWS),)),
        ],
        compiler_params=pltpu.CompilerParams(collective_id=0, has_side_effects=True, vmem_limit_bytes=28 * 2**20),
    )(outer_param, inner)


def body(outer_param, momentum, inner_weights):
    pseudo, factor = all_reduce(outer_param, inner_weights[0])
    grad = factor[0, 0] * pseudo
    new_momentum = 0.9 * momentum + grad
    new_outer = outer_param - 0.7 * (grad + 0.9 * new_momentum)
    merged = (0.5 * inner_weights.astype(jnp.float32) + 0.5 * new_outer[None]).astype(jnp.bfloat16)
    return (new_outer, new_momentum, merged)


def solution(mesh):
    in_specs = (P("fsdp", None), P("fsdp", None), P("replica", "fsdp", None))
    out_specs = (P("fsdp", None), P("fsdp", None), P("replica", "fsdp", None))
    return jax.shard_map(body, mesh=mesh, in_specs=in_specs, out_specs=out_specs, check_vma=False)
```

time: 199 us -> 65.2 us (0.33); the launches traced: 196 us -> 65 us
  waiting for transfers between devices: 159 us -> 0 us
  Pallas kernels: 0 us -> 55.9 us
  between operations: 14.7 us -> 0.65 us
  blocking collectives: 10.6 us -> 0 us
  other arithmetic: 11.3 us -> 5.08 us
  local copies, waits for them, and re-layouts: 0.01 us -> 3.32 us
    psum x1 -> x0, waiting for transfers between devices: 159 us -> none  [body(): pseudo = lax.psum(local, 'replica') / count]
    pallas_call x0 -> x1, Pallas kernels: none -> 55.9 us  [all_reduce(): pl.pallas_call(kernel, out_shape=(jax.ShapeDtypeStruct((ROWS, COLS), jnp....]
    psum x1 -> x0, blocking collectives: 10.6 us -> none  [body(): squares = lax.psum(jnp.sum(pseudo * pseudo), 'fsdp')]
    sub x1 -> x0, other arithmetic: 3.35 us -> none  [body(): local = outer_param - inner_weights[0].astype(jnp.float32)]
    unnamed x4 -> x8, local copies, waits for them, and re-layouts: 0.01 us -> 2.82 us
    reduce_sum x1 -> x0, other arithmetic: 2.73 us -> none  [body(): squares = lax.psum(jnp.sum(pseudo * pseudo), 'fsdp')]
  transfers between devices with their start and end apart: 1 -> 0, of which waited for: 1 -> 0; matrix products, arithmetic and copies ran while one was open for 0% -> 0% of each run, Pallas kernels for 0% -> 0%
where the time goes in v1:
time: 65.2 us; the launch traced here: 65 us
  Pallas kernels  55.9 us (86%)
  other arithmetic  5.08 us (8%)
  local copies, waits for them, and re-layouts  3.32 us (5%)
    pallas_call x1, Pallas kernels, all_reduce(): pl.pallas_call(kernel, out_shape=(jax.ShapeDtypeStruct((ROWS, COLS), jnp....  55.9 us
    convert_element_type x1, other arithmetic, body(): (0.5 * inner_weights.astype(jnp.float32) + 0.5 * new_outer[None]).astype(...  5.08 us
    unnamed x8, local copies, waits for them, and re-layouts  2.82 us

profile of v1, /device:TPU:2, one launch (start us, length us, event | category | flops | bytes accessed | tf_op | source)
XLA Modules:
  0.0 65.0 jit_solution(13109431986899746475)
XLA Ops:
  0.6 0.0 copy-start
  0.6 1.6 %copy-done = f32[64,8192]{1,0:T(8,128)S(1)} copy-done((f32[64,8192]{1,0:T(8,128)S(1)}, f32[64,8192]{1,0:T(8,128)}, u32[]{:S(2)}) %copy-start) | copy-done | bytes 2097176
  2.2 0.0 copy-start.2
  2.2 1.2 %copy-done.2 = bf16[1,64,8192]{2,1,0:T(8,128)(2,1)S(1)} copy-done((bf16[1,64,8192]{2,1,0:T(8,128)(2,1)S(1)}, bf16[1,64,8192]{2,1,0:T(8,128)(2,1)}, u32[]{:S(2)}) %copy-start.2) | copy-done | bytes 1048600
  3.4 0.0 copy-start.1
  3.4 0.0 copy-start.3
  3.5 55.9 %shard_map.58 = (f32[64,8192]{1,0:T(8,128)S(1)}, f32[8,128]{1,0:T(8,128)S(1)}) custom-call(f32[64,8192]{1,0:T(8,128)S(1)} %copy-done, bf16[64,8192]{1,0:T(8,128)(2,1)S(1)} %bitcast.8), custom_call_target="tpu_custom_call" | custom-call | tf_op jit(solution)/shard_map/pallas_call | solution.py:288
  59.4 0.5 slice.3
  59.9 0.0 copy-done.1
  59.9 0.0 copy-done.3
  59.9 5.1 %fusion.1 = (bf16[1,64,8192]{2,1,0:T(8,128)(2,1)}, f32[64,8192]{1,0:T(8,128)}, f32[64,8192]{1,0:T(8,128)}) fusion(bf16[1,64,8192]{2,1,0:T(8,128)(2,1)S(1)} %copy-done.3, f32[64,8192]{1,0:T(8,128)S(1)} %copy-done.1, f32[64,8192]{1,0:T(8,128)S(1)} %get-tuple-element.6, f32[]{:T(128)} %bitcast.1, f32[64,8192]{1,0:T(8,128)} %param.4), kind=kLoop, calls=%fused_computation.2 | loop fusion | flops 5767168 | bytes 12582916 | tf_op jit(solution)/shard_map/convert_element_type | solution.py:313
Async XLA Ops:
  0.6 1.6 %copy-start = (f32[64,8192]{1,0:T(8,128)S(1)}, f32[64,8192]{1,0:T(8,128)}, u32[]{:S(2)}) copy-start(f32[64,8192]{1,0:T(8,128)} %outer_hbm.1) | copy-start | bytes 6291460
  2.2 1.2 %copy-start.2 = (bf16[1,64,8192]{2,1,0:T(8,128)(2,1)S(1)}, bf16[1,64,8192]{2,1,0:T(8,128)(2,1)}, u32[]{:S(2)}) copy-start(bf16[1,64,8192]{2,1,0:T(8,128)(2,1)} %param.5) | copy-start | bytes 3145732
  3.4 56.4 %copy-start.1 = (f32[64,8192]{1,0:T(8,128)S(1)}, f32[64,8192]{1,0:T(8,128)}, u32[]{:S(2)}) copy-start(f32[64,8192]{1,0:T(8,128)} %outer_hbm.1) | copy-start | bytes 6291460
  3.4 56.4 %copy-start.3 = (bf16[1,64,8192]{2,1,0:T(8,128)(2,1)S(1)}, bf16[1,64,8192]{2,1,0:T(8,128)(2,1)}, u32[]{:S(2)}) copy-start(bf16[1,64,8192]{2,1,0:T(8,128)(2,1)} %param.5) | copy-start | bytes 3145732

commit v2 on v0

v2 whole, which is shorter than its diff:
```python
import jax
import jax.numpy as jnp
from jax import lax
from jax.experimental import pallas as pl
from jax.experimental.pallas import tpu as pltpu
from jax.sharding import PartitionSpec as P

MESH = pl.DeviceIdType.MESH
NY, NZ, NX = 4, 8, 4
ROWS, COLS = 64, 8192
REPLICAS = 32
ENTRIES = 512 * 8192
FLOWS = (
    (0, 1024, "yz", 2, 2, "zy", 2, 1),
    (1024, 2048, "zy", 3, 1, "zy", 2, 2),
    (3072, 1024, "yz", 2, 2, "yz", 3, 1),
    (4096, 1024, "yz", 1, 2, "yz", 3, 1),
    (5120, 2048, "yz", 2, 2, "yz", 3, 1),
    (7168, 1024, "zy", 2, 1, "zy", 2, 1),
)
ORDER = (
    0, 2, 3, 1, 4, 5, 0, 2, 1, 3, 5, 4, 0, 1, 2, 5, 4, 3, 0, 1, 2, 5, 4, 6, 3, 0, 1, 2, 5, 4, 6, 3, 0, 2, 1, 4, 5, 3, 2, 6, 4, 1, 3, 0, 2, 6, 1, 4,
)
MAX_GROUPS = 47
FROM_Y = {1: 0, -1: 1, 2: 2}
FROM_Z = {1: 3, -1: 4, 2: 5, -2: 6, 3: 7, -3: 8, 4: 9}
PLANES = 10
BOTH = (1, -1)
STAGES = (
    [dict(dx=x, dc=c) for x in (2, 1, 3, 0) for c in (1, 0) if x or c],
    [dict(dz=d) for d in (4, 3, 5, 2, 6, 1, 7)],
    [dict(dy=d) for d in (2, 1, 3)],
)
PEERS = [d for stage in STAGES for d in stage]


class Group:
    def __init__(self, sem):
        self.sem = sem
        self.tiles = 0


class AllReduce:
    def __init__(self, acc, got, full, send_sems, recv_sems):
        self.acc, self.got, self.full = acc, got, full
        self.send_sems, self.recv_sems = send_sems, recv_sems
        r, f = lax.axis_index("replica"), lax.axis_index("fsdp")
        self.y, self.z = r // NZ, r % NZ
        self.x, self.c = f // 2, f % 2
        self.groups = 0
        self.sent = [0, 0]
        self.squares = []

    def device(self, dy=0, dz=0, dx=0, dc=0):
        y, z, x, c = self.y, self.z, self.x, self.c
        y = lax.rem(y + (dy % NY), NY) if dy else y
        z = lax.rem(z + (dz % NZ), NZ) if dz else z
        x = lax.rem(x + (dx % NX), NX) if dx else x
        c = 1 - c if dc else c
        return (y * NZ + z, x * 2 + c)

    def group(self):
        assert self.groups < MAX_GROUPS
        self.groups += 1
        return Group(self.groups - 1)

    def copy(self, group, tiles, src, dst, small=0, **to):
        group.tiles += tiles
        self.sent[small] += tiles
        pltpu.make_async_remote_copy(
            src_ref=src, dst_ref=dst, send_sem=self.send_sems.at[small], recv_sem=self.recv_sems.at[group.sem],
            device_id=self.device(**to), device_id_type=MESH).start()

    def bytes_of(self, tiles):
        for p in range(1, PLANES + 1):
            for r in range(1, 9):
                if tiles % (p * r) == 0 and tiles // (p * r) <= COLS // 128:
                    return self.got.at[pl.ds(0, p), pl.ds(0, 8 * r), pl.ds(0, tiles // (p * r) * 128)]
        raise NotImplementedError

    def waiter(self, tiles, small, sem):
        place = self.bytes_of(tiles)
        return pltpu.make_async_remote_copy(
            src_ref=place, dst_ref=place, send_sem=self.send_sems.at[small], recv_sem=self.recv_sems.at[sem],
            device_id=self.device(dc=1), device_id_type=MESH)

    def wait(self, group):
        self.waiter(group.tiles, 0, group.sem).wait_recv()

    def drain(self):
        for small, tiles in enumerate(self.sent):
            self.waiter(tiles, small, 0).wait_send()

    @staticmethod
    def at(region):
        r, n, c, w = region
        return (pl.ds(r, n), pl.ds(c, w))

    def push(self, group, region, plane, **to):
        rs, cs = self.at(region)
        self.copy(group, region[1] * region[3] // 1024, self.acc.at[rs, cs], self.got.at[plane, rs, cs], **to)

    def push_z(self, group, region, d):
        self.push(group, region, FROM_Z[d], dz=d)

    def push_y(self, group, region, d):
        self.push(group, region, FROM_Y[d], dy=d)

    def pass_on(self, group, region, **to):
        rs, cs = self.at(region)
        self.copy(group, region[1] * region[3] // 1024, self.full.at[rs, cs], self.full.at[rs, cs], **to)

    def add(self, region, planes):
        rs, cs = self.at(region)
        total = self.acc[rs, cs]
        for p in planes:
            total = total + self.got[p, rs, cs]
        self.acc[rs, cs] = total

    def finish(self, region):
        rs, cs = self.at(region)
        pseudo = self.acc[rs, cs] / REPLICAS
        self.full[rs, cs] = pseudo
        self.squares.append(sum(pseudo[:, i:i + 128] * pseudo[:, i:i + 128] for i in range(0, region[3], 128)))

    def shard(self, d, c, w):
        g = lax.rem(self.z + (d % NZ), NZ) if d % NZ else self.z
        return (pl.multiple_of(g * 8, 8), 8, c, w)

    def half_shard(self, d, c, w, s):
        h = w // 2
        return self.shard(d, c if s > 0 else c + h, h)

    def scatter_z(self, c, w, depth):
        sh = lambda d: self.shard(d, c, w)
        half = lambda d, s: self.half_shard(d, c, w, s)
        g = self.group()
        if depth == 1:
            for d in (4, 3, -3, 2, -2, 1, -1):
                self.push_z(g, sh(d), d)
            yield g
            self.wait(g)
            self.add(sh(0), list(FROM_Z.values()))
            return
        if depth == 4:
            for s in BOTH:
                self.push_z(g, half(4, s), s)
            yield g
            self.wait(g)
            g = self.group()
            for s in BOTH:
                self.add(half(3 * s, s), [FROM_Z[s]])
                self.push_z(g, sh(3 * s), s)
            yield g
            self.wait(g)
            g = self.group()
            for s in BOTH:
                self.add(sh(2 * s), [FROM_Z[s]])
                self.push_z(g, sh(2 * s), s)
        else:
            for s in BOTH:
                self.push_z(g, half(4, s), 2 * s)
            for s in BOTH:
                self.push_z(g, sh(3 * s), s)
            after = self.group()
            if depth == 2:
                for s in BOTH:
                    self.push_z(after, sh(s), s)
            yield g
            self.wait(g)
            for s in BOTH:
                self.add(sh(2 * s), [FROM_Z[s]])
                self.add(half(2 * s, s), [FROM_Z[2 * s]])
                self.push_z(after, sh(2 * s), s if depth == 3 else 2 * s)
            g = after
            if depth == 2:
                yield g
                self.wait(g)
                self.add(sh(0), [FROM_Z[d] for d in (1, -1, 2, -2)])
                return
        yield g
        self.wait(g)
        g = self.group()
        for s in BOTH:
            self.add(sh(s), [FROM_Z[s]])
            self.push_z(g, sh(s), s)
        yield g
        self.wait(g)
        self.add(sh(0), [FROM_Z[1], FROM_Z[-1]])

    def gather_z(self, c, w, depth):
        sh = lambda d: self.shard(d, c, w)
        half = lambda d, s: self.half_shard(d, c, w, s)
        g = self.group()
        if depth == 1:
            for d in (4, 3, -3, 2, -2, 1, -1):
                self.pass_on(g, sh(0), dz=d)
            yield g
            self.wait(g)
            return
        if depth == 2:
            for s in BOTH:
                self.pass_on(g, sh(0), dz=2 * s)
            last = self.group()
            for s in BOTH:
                self.pass_on(last, sh(0), dz=s)
            yield g
            self.wait(g)
            for s in BOTH:
                self.pass_on(last, half(-2 * s, s), dz=2 * s)
            for s in BOTH:
                self.pass_on(last, sh(-2 * s), dz=s)
            yield last
            self.wait(last)
            return
        for s in BOTH:
            self.pass_on(g, sh(0), dz=s)
        yield g
        self.wait(g)
        g = self.group()
        for s in BOTH:
            self.pass_on(g, sh(-s), dz=s)
        yield g
        self.wait(g)
        g = self.group()
        if depth == 3:
            for s in BOTH:
                self.pass_on(g, half(-2 * s, s), dz=2 * s)
        for s in BOTH:
            self.pass_on(g, sh(-2 * s), dz=s)
        yield g
        self.wait(g)
        if depth == 4:
            g = self.group()
            for s in BOTH:
                self.pass_on(g, half(-3 * s, s), dz=s)
            yield g
            self.wait(g)

    def quarter(self, d, r, n, c, w):
        q = lax.rem(self.y + (d % NY), NY) if d % NY else self.y
        return (r, n, pl.multiple_of(c + q * (w // 4), 128), w // 4)

    def half_quarter(self, d, r, n, c, w, s):
        r, n, c, w = self.quarter(d, r, n, c, w)
        if n > 8:
            return (r if s > 0 else r + n // 2, n // 2, c, w)
        return (r, n, c if s > 0 else pl.multiple_of(c + w // 2, 128), w // 2)

    def scatter_y(self, r, n, c, w, depth):
        part = lambda d: self.quarter(d, r, n, c, w)
        half = lambda d, s: self.half_quarter(d, r, n, c, w, s)
        g = self.group()
        if depth == 1:
            for d in (2, 1, -1):
                self.push_y(g, part(d), d)
            yield g
            self.wait(g)
            self.add(part(0), list(FROM_Y.values()))
            return
        for s in BOTH:
            self.push_y(g, half(2, s), s)
        yield g
        self.wait(g)
        g = self.group()
        for s in BOTH:
            self.add(half(s, s), [FROM_Y[s]])
            self.push_y(g, part(s), s)
        yield g
        self.wait(g)
        self.add(part(0), [FROM_Y[s] for s in BOTH])

    def gather_y(self, r, n, c, w, depth):
        part = lambda d: self.quarter(d, r, n, c, w)
        g = self.group()
        for d in (2, 1, -1) if depth == 1 else BOTH:
            self.pass_on(g, part(0), dy=d)
        yield g
        self.wait(g)
        if depth == 2:
            g = self.group()
            for s in BOTH:
                self.pass_on(g, self.half_quarter(-s, r, n, c, w, s), dy=s)
            yield g
            self.wait(g)

    def flow(self, c, w, scatter, scatter_z, scatter_y, gather, gather_z, gather_y):
        r, n, q, v = self.shard(0, *self.quarter(0, 0, 8, c, w)[2:])
        if scatter == "zy":
            yield from self.scatter_z(c, w, scatter_z)
            yield from self.scatter_y(r, n, c, w, scatter_y)
        else:
            yield from self.scatter_y(0, ROWS, c, w, scatter_y)
            yield from self.scatter_z(q, v, scatter_z)
        self.finish((r, n, q, v))
        if gather == "yz":
            yield from self.gather_y(r, n, c, w, gather_y)
            yield from self.gather_z(c, w, gather_z)
        else:
            yield from self.gather_z(q, v, gather_z)
            yield from self.gather_y(0, ROWS, c, w, gather_y)

    def clip(self, factor, sums, parts):
        while len(self.squares) < len(FLOWS):
            yield None
        total = sum(self.squares)
        n = 0
        for i, stage in enumerate(STAGES):
            sums[i] = total
            g = self.group()
            for j, d in enumerate(stage):
                self.copy(g, 1, sums.at[i], parts.at[n + j], small=1, **d)
            yield g
            self.wait(g)
            total = total + sum(parts[n + j] for j in range(len(stage)))
            n += len(stage)
        mean = jnp.full((8, 128), jnp.sum(total)) / ENTRIES
        factor[...] = jnp.minimum(1.0, 0.5 / jnp.sqrt(mean + 1e-6))


def exchange(outer_hbm, inner_hbm, momentum_hbm, full, factor, outer, inner, momentum, acc, got, sums, parts, send_sems, recv_sems, load_sems):
    ar = AllReduce(acc, got, full, send_sems, recv_sems)
    barrier = pltpu.get_barrier_semaphore()
    for p in PEERS:
        pl.semaphore_signal(barrier, inc=1, device_id=ar.device(**p), device_id_type=MESH)
    loads = []
    for i, (c, w, *_) in enumerate(FLOWS):
        cs = pl.ds(c, w)
        for j, (src, dst) in enumerate(((outer_hbm, outer), (inner_hbm, inner))):
            loads.append(pltpu.make_async_copy(src.at[:, cs], dst.at[:, cs], load_sems.at[2 * i + j]))
            loads[-1].start()
    loads.append(pltpu.make_async_copy(momentum_hbm, momentum, load_sems.at[len(loads)]))
    loads[-1].start()
    flows = []
    for i, (c, w, *plan) in enumerate(FLOWS):
        loads[2 * i].wait()
        loads[2 * i + 1].wait()
        acc[:, pl.ds(c, w)] = outer[:, pl.ds(c, w)] - inner[:, pl.ds(c, w)].astype(jnp.float32)
        if i == 0:
            pl.semaphore_wait(barrier, len(PEERS))
        flows.append(ar.flow(c, w, *plan))
        next(flows[-1])
    flows.append(ar.clip(factor, sums, parts))
    for i in ORDER:
        next(flows[i], None)
    while flows:
        flows = [g for g in flows if next(g, flows) is not flows]
    ar.drain()
    loads[-1].wait()


def all_reduce(outer_param, inner, momentum):
    array = pltpu.VMEM((ROWS, COLS), jnp.float32)
    operands = [pltpu.with_memory_space_constraint(a, pltpu.HBM) for a in (outer_param, inner, momentum)]
    return pl.pallas_call(
        exchange,
        out_shape=(array, pltpu.VMEM((8, 128), jnp.float32), array, pltpu.VMEM((ROWS, COLS), jnp.bfloat16), array),
        in_specs=[pl.BlockSpec(memory_space=pl.ANY)] * 3,
        out_specs=(pl.BlockSpec(memory_space=pltpu.VMEM),) * 5,
        scratch_shapes=[
            pltpu.VMEM((ROWS, COLS), jnp.float32),
            pltpu.VMEM((PLANES, ROWS, COLS), jnp.float32),
            pltpu.VMEM((len(STAGES), 8, 128), jnp.float32),
            pltpu.VMEM((len(PEERS), 8, 128), jnp.float32),
            pltpu.SemaphoreType.DMA((2,)),
            pltpu.SemaphoreType.DMA((MAX_GROUPS,)),
            pltpu.SemaphoreType.DMA((2 * len(FLOWS) + 1,)),
        ],
        compiler_params=pltpu.CompilerParams(collective_id=0, has_side_effects=True, vmem_limit_bytes=32 * 2**20),
    )(*operands)


BLOCK = (16, 4096)
STRIP = 512


def update(pseudo, factor, outer, inner, momentum, new_outer_hbm, new_momentum_hbm, merged_hbm, new_outer, new_momentum, merged, sems):
    f = jnp.broadcast_to(factor[0:1, 0:1], (BLOCK[0], STRIP))
    stores = []
    for r in range(0, ROWS, BLOCK[0]):
        for c in range(0, COLS, BLOCK[1]):
            rs = pl.ds(r, BLOCK[0])

            @pl.loop(c, c + BLOCK[1], step=STRIP)
            def _(i):
                cs = pl.ds(pl.multiple_of(i, STRIP), STRIP)
                grad = f * pseudo[rs, cs]
                m = 0.9 * momentum[rs, cs] + grad
                o = outer[rs, cs] - 0.7 * (grad + 0.9 * m)
                new_momentum[rs, cs] = m
                new_outer[rs, cs] = o
                merged[rs, cs] = (0.5 * inner[rs, cs].astype(jnp.float32) + 0.5 * o).astype(jnp.bfloat16)

            cs = pl.ds(c, BLOCK[1])
            for src, dst in ((new_outer, new_outer_hbm), (new_momentum, new_momentum_hbm), (merged, merged_hbm)):
                stores.append(pltpu.make_async_copy(src.at[rs, cs], dst.at[rs, cs], sems.at[len(stores)]))
                stores[-1].start()
    for s in stores:
        s.wait()


def outer_update(pseudo, factor, outer, inner, momentum):
    shapes = ((ROWS, COLS), jnp.float32), ((ROWS, COLS), jnp.float32), ((ROWS, COLS), jnp.bfloat16)
    return pl.pallas_call(
        update,
        out_shape=[pltpu.HBM(*s) for s in shapes],
        in_specs=[pl.BlockSpec(memory_space=pltpu.VMEM)] * 5,
        out_specs=[pl.BlockSpec(memory_space=pltpu.HBM)] * 3,
        scratch_shapes=[pltpu.VMEM(*s) for s in shapes] + [pltpu.SemaphoreType.DMA((3 * (ROWS // BLOCK[0]) * (COLS // BLOCK[1]),))],
        compiler_params=pltpu.CompilerParams(vmem_limit_bytes=16 * 2**20),
    )(pseudo, factor, outer, inner, momentum)


def body(outer_param, momentum, inner_weights):
    inner = inner_weights[0]
    new_outer, new_momentum, merged = outer_update(*all_reduce(outer_param, inner, momentum))
    return (new_outer, new_momentum, merged[None])


def solution(mesh):
    in_specs = (P("fsdp", None), P("fsdp", None), P("replica", "fsdp", None))
    out_specs = (P("fsdp", None), P("fsdp", None), P("replica", "fsdp", None))
    return jax.shard_map(body, mesh=mesh, in_specs=in_specs, out_specs=out_specs, check_vma=False)
```

time: 199 us -> 50.1 us (0.25); the launches traced: 196 us -> 49.9 us
  waiting for transfers between devices: 159 us -> 0 us
  Pallas kernels: 0 us -> 49.2 us
  between operations: 14.7 us -> 0.64 us
  other arithmetic: 11.3 us -> 0 us
  blocking collectives: 10.6 us -> 0 us
    psum x1 -> x0, waiting for transfers between devices: 159 us -> none  [body(): pseudo = lax.psum(local, 'replica') / count]
    pallas_call x0 -> x2, Pallas kernels: none -> 49.2 us  [the longest x1 46.5 us: all_reduce(): pl.pallas_call(exchange, out_shape=(array, pltpu.VMEM((8, 128), jnp.float...]
    psum x1 -> x0, blocking collectives: 10.6 us -> none  [body(): squares = lax.psum(jnp.sum(pseudo * pseudo), 'fsdp')]
    convert_element_type x1 -> x0, other arithmetic: 5.21 us -> none  [body(): (0.5 * inner_weights.astype(jnp.float32) + 0.5 * new_outer[None]).astype(...]
    sub x1 -> x0, other arithmetic: 3.35 us -> none  [body(): local = outer_param - inner_weights[0].astype(jnp.float32)]
    reduce_sum x1 -> x0, other arithmetic: 2.73 us -> none  [body(): squares = lax.psum(jnp.sum(pseudo * pseudo), 'fsdp')]
  transfers between devices with their start and end apart: 1 -> 0, of which waited for: 1 -> 0; matrix products, arithmetic and copies ran while one was open for 0% -> 0% of each run, Pallas kernels for 0% -> 0%
where the time goes in v2:
time: 50.1 us; the launch traced here: 49.9 us
  Pallas kernels  49.2 us (98%)
  between operations  0.64 us (1%)
    pallas_call x1, Pallas kernels, all_reduce(): pl.pallas_call(exchange, out_shape=(array, pltpu.VMEM((8, 128), jnp.float...  46.5 us
    pallas_call x1, Pallas kernels, outer_update(): pl.pallas_call(update, out_shape=[pltpu.HBM(*s) for s in shapes], in_spec...  2.69 us

profile of v2, /device:TPU:2, one launch (start us, length us, event | category | flops | bytes accessed | tf_op | source)
XLA Modules:
  0.0 49.9 jit_solution(1514040624345417414)
XLA Ops:
  0.6 46.5 %shard_map.58 = (f32[64,8192]{1,0:T(8,128)S(1)}, f32[8,128]{1,0:T(8,128)S(1)}, f32[64,8192]{1,0:T(8,128)S(1)}, bf16[64,8192]{1,0:T(8,128)(2,1)S(1)}, f32[64,8192]{1,0:T(8,128)S(1)}) custom-call(f32[64,8192]{1,0:T(8,128)} %outer_hbm.1, bf16[64,8192]{1,0:T(8,128)(2,1)} %bitcast.2, f32[64,8192]{1,0:T(8,128)} %momentum_hbm.1), custom_call_target="tpu_custom_call" | custom-call | tf_op jit(solution)/shard_map/pallas_call | solution.py:355
  47.2 2.7 %shard_map.59 = (f32[64,8192]{1,0:T(8,128)}, f32[64,8192]{1,0:T(8,128)}, bf16[64,8192]{1,0:T(8,128)(2,1)}) custom-call(f32[64,8192]{1,0:T(8,128)S(1)} %get-tuple-element.11.pseudo, f32[8,128]{1,0:T(8,128)S(1)} %get-tuple-element.12.factor, f32[64,8192]{1,0:T(8,128)S(1)} %get-tuple-element.13.outer, bf16[64,8192]{1,0:T(8,128)(2,1)S(1)} %get-tuple-element.14.inner, ...), custom_call_target="tpu_custom_call" | custom-call | tf_op jit(solution)/shard_map/pallas_call | solution.py:404

commit v3 on v2

--- a/solution.py
+++ b/solution.py
@@ -11,27 +11,32 @@
 REPLICAS = 32
 ENTRIES = 512 * 8192
 FLOWS = (
-    (0, 1024, "yz", 2, 2, "zy", 2, 1),
-    (1024, 2048, "zy", 3, 1, "zy", 2, 2),
-    (3072, 1024, "yz", 2, 2, "yz", 3, 1),
-    (4096, 1024, "yz", 1, 2, "yz", 3, 1),
-    (5120, 2048, "yz", 2, 2, "yz", 3, 1),
-    (7168, 1024, "zy", 2, 1, "zy", 2, 1),
+    (0, 2048, "yz", 2, 2, "yz", 3, 1),
+    (2048, 1024, "zy", 3, 1, "zy", 1, 2),
+    (3072, 2048, "yz", 2, 2, "yz", 3, 1),
+    (5120, 2048, "zy", 3, 1, "zy", 1, 1),
+    (7168, 1024, "yz", 2, 2, "zy", 2, 1),
 )
 ORDER = (
-    0, 2, 3, 1, 4, 5, 0, 2, 1, 3, 5, 4, 0, 1, 2, 5, 4, 3, 0, 1, 2, 5, 4, 6, 3, 0, 1, 2, 5, 4, 6, 3, 0, 2, 1, 4, 5, 3, 2, 6, 4, 1, 3, 0, 2, 6, 1, 4,
+    0, 1, 3, 2, 4, 0, 1, 2, 3, 4, 1, 0, 3, 2, 1, 4, 0, 3, 2, 1, 4, 0, 3, 2, 4, 5, 0, 1, 2, 4, 3, 0, 1, 5, 2, 4, 0, 1, 5, 2, 3, 0, 4, 5, 2,
 )
-MAX_GROUPS = 47
+MAX_GROUPS = 39
 FROM_Y = {1: 0, -1: 1, 2: 2}
 FROM_Z = {1: 3, -1: 4, 2: 5, -2: 6, 3: 7, -3: 8, 4: 9}
-PLANES = 10
+SPARE = (5, 6, 7, 8, 9, 10)
+PLANES = 11
 BOTH = (1, -1)
 STAGES = (
+    [dict(dz=d) for d in (4, 3, 5, 2, 6, 1, 7)],
     [dict(dx=x, dc=c) for x in (2, 1, 3, 0) for c in (1, 0) if x or c],
-    [dict(dz=d) for d in (4, 3, 5, 2, 6, 1, 7)],
     [dict(dy=d) for d in (2, 1, 3)],
 )
 PEERS = [d for stage in STAGES for d in stage]
+
+
+CORNERS = sorted({(2 if z == 2 else 1) for _, _, *p in FLOWS for z, y in ((p[1], p[2]), (p[4], p[5])) if y == 0})
+PEERS += [dict(dz=s * d, dy=q) for d in CORNERS for s in BOTH for q in (2, 1, -1)]
+PEERS.sort(key=lambda p: -sum(min(d % n, -d % n) for d, n in ((p.get("dz", 0), NZ), (p.get("dy", 0), NY), (p.get("dx", 0), NX))))
 
 
 class Group:
@@ -45,19 +50,19 @@
         self.acc, self.got, self.full = acc, got, full
         self.send_sems, self.recv_sems = send_sems, recv_sems
         r, f = lax.axis_index("replica"), lax.axis_index("fsdp")
-        self.y, self.z = r // NZ, r % NZ
-        self.x, self.c = f // 2, f % 2
+        y, z, x = r // NZ, r % NZ, f // 2
+        self.c = f % 2
+        self.ys = [y] + [lax.rem(y + d, NY) for d in range(1, NY)]
+        self.zs = [z] + [lax.rem(z + d, NZ) for d in range(1, NZ)]
+        self.xs = [x] + [lax.rem(x + d, NX) for d in range(1, NX)]
+        self.rows = [pl.multiple_of(g * 8, 8) for g in self.zs]
         self.groups = 0
         self.sent = [0, 0]
         self.squares = []
 
     def device(self, dy=0, dz=0, dx=0, dc=0):
-        y, z, x, c = self.y, self.z, self.x, self.c
-        y = lax.rem(y + (dy % NY), NY) if dy else y
-        z = lax.rem(z + (dz % NZ), NZ) if dz else z
-        x = lax.rem(x + (dx % NX), NX) if dx else x
-        c = 1 - c if dc else c
-        return (y * NZ + z, x * 2 + c)
+        c = 1 - self.c if dc else self.c
+        return (self.ys[dy % NY] * NZ + self.zs[dz % NZ], self.xs[dx % NX] * 2 + c)
 
     def group(self):
         assert self.groups < MAX_GROUPS
@@ -123,18 +128,59 @@
         self.full[rs, cs] = pseudo
         self.squares.append(sum(pseudo[:, i:i + 128] * pseudo[:, i:i + 128] for i in range(0, region[3], 128)))
 
+    def finish_rows(self, region, mine):
+        rs, cs = self.at(region)
+        even = self.acc[rs, cs] + self.got[FROM_Y[2], rs, cs]
+        odd = self.got[FROM_Y[1], rs, cs] + self.got[FROM_Y[-1], rs, cs]
+        self.full[rs, cs] = (even + odd) / REPLICAS
+        rs, cs = self.at(mine)
+        pseudo = self.full[rs, cs]
+        self.squares.append(sum(pseudo[:, i:i + 128] * pseudo[:, i:i + 128] for i in range(0, mine[3], 128)))
+
     def shard(self, d, c, w):
-        g = lax.rem(self.z + (d % NZ), NZ) if d % NZ else self.z
-        return (pl.multiple_of(g * 8, 8), 8, c, w)
+        return (self.rows[d % NZ], 8, c, w)
 
     def half_shard(self, d, c, w, s):
         h = w // 2
         return self.shard(d, c if s > 0 else c + h, h)
 
-    def scatter_z(self, c, w, depth):
+    def push_corners(self, group, c, w, d):
+        for q in (2, 1, -1, 0):
+            for s in BOTH:
+                plane = FROM_Z[s * d] if q == 0 else SPARE[(1 - s) // 2 * 3 + q % NY - 1]
+                self.push(group, self.quarter(q, *self.shard(s * d, c, w)), plane, dz=s * d, dy=q)
+
+    def push_rows(self, group, c, w):
+        for q in (2, 1, -1):
+            self.push_y(group, self.quarter(q, *self.shard(0, c, w)), q)
+
+    def add_corners(self, c, w, d):
+        self.add(self.quarter(0, *self.shard(0, c, w)), [FROM_Z[d], FROM_Z[-d], *SPARE, *FROM_Y.values()])
+
+    def scatter_z(self, c, w, depth, merged=False):
         sh = lambda d: self.shard(d, c, w)
         half = lambda d, s: self.half_shard(d, c, w, s)
         g = self.group()
+        if merged and depth == 2:
+            for s in BOTH:
+                self.push_z(g, half(4, s), 2 * s)
+            for s in BOTH:
+                self.push_z(g, sh(3 * s), s)
+            for s in BOTH:
+                self.push_z(g, sh(s), s)
+            yield g
+            self.wait(g)
+            g = self.group()
+            for s in BOTH:
+                self.add(sh(2 * s), [FROM_Z[s]])
+                self.add(half(2 * s, s), [FROM_Z[2 * s]])
+            self.push_corners(g, c, w, 2)
+            self.add(sh(0), [FROM_Z[s] for s in BOTH])
+            self.push_rows(g, c, w)
+            yield g
+            self.wait(g)
+            self.add_corners(c, w, 2)
+            return
         if depth == 1:
             for d in (4, 3, -3, 2, -2, 1, -1):
                 self.push_z(g, sh(d), d)
@@ -178,8 +224,19 @@
                 self.wait(g)
                 self.add(sh(0), [FROM_Z[d] for d in (1, -1, 2, -2)])
                 return
-        yield g
-        self.wait(g)
+        if merged:
+            last = self.group()
+            self.push_rows(last, c, w)
+        yield g
+        self.wait(g)
+        if merged:
+            for s in BOTH:
+                self.add(sh(s), [FROM_Z[s]])
+            self.push_corners(last, c, w, 1)
+            yield last
+            self.wait(last)
+            self.add_corners(c, w, 1)
+            return
         g = self.group()
         for s in BOTH:
             self.add(sh(s), [FROM_Z[s]])
@@ -188,17 +245,39 @@
         self.wait(g)
         self.add(sh(0), [FROM_Z[1], FROM_Z[-1]])
 
-    def gather_z(self, c, w, depth):
+    def gather_z(self, c, w, depth, merged=False):
         sh = lambda d: self.shard(d, c, w)
         half = lambda d, s: self.half_shard(d, c, w, s)
         g = self.group()
+        if merged:
+            mine = self.quarter(0, *sh(0))
+            d = 2 if depth == 2 else 1
+            for q in (2, 1, -1, 0):
+                for s in BOTH:
+                    self.pass_on(g, mine, dz=s * d, dy=q)
+                if q:
+                    self.pass_on(g, mine, dy=q)
+            yield g
+            self.wait(g)
+            g = self.group()
+            if depth == 2:
+                for s in BOTH:
+                    self.pass_on(g, half(-2 * s, s), dz=2 * s)
+                for s in BOTH:
+                    self.pass_on(g, sh(0), dz=s)
+                    self.pass_on(g, sh(-2 * s), dz=s)
+                yield g
+                self.wait(g)
+                return
+            for s in BOTH:
+                self.pass_on(g, sh(-s), dz=s)
         if depth == 1:
             for d in (4, 3, -3, 2, -2, 1, -1):
                 self.pass_on(g, sh(0), dz=d)
             yield g
             self.wait(g)
             return
-        if depth == 2:
+        if depth == 2 and not merged:
             for s in BOTH:
                 self.pass_on(g, sh(0), dz=2 * s)
             last = self.group()
@@ -213,13 +292,14 @@
             yield last
             self.wait(last)
             return
-        for s in BOTH:
-            self.pass_on(g, sh(0), dz=s)
-        yield g
-        self.wait(g)
-        g = self.group()
-        for s in BOTH:
-            self.pass_on(g, sh(-s), dz=s)
+        if not merged:
+            for s in BOTH:
+                self.pass_on(g, sh(0), dz=s)
+            yield g
+            self.wait(g)
+            g = self.group()
+            for s in BOTH:
+                self.pass_on(g, sh(-s), dz=s)
         yield g
         self.wait(g)
         g = self.group()
@@ -238,8 +318,7 @@
             self.wait(g)
 
     def quarter(self, d, r, n, c, w):
-        q = lax.rem(self.y + (d % NY), NY) if d % NY else self.y
-        return (r, n, pl.multiple_of(c + q * (w // 4), 128), w // 4)
+        return (r, n, pl.multiple_of(c + self.ys[d % NY] * (w // 4), 128), w // 4)
 
     def half_quarter(self, d, r, n, c, w, s):
         r, n, c, w = self.quarter(d, r, n, c, w)
@@ -287,15 +366,26 @@
     def flow(self, c, w, scatter, scatter_z, scatter_y, gather, gather_z, gather_y):
         r, n, q, v = self.shard(0, *self.quarter(0, 0, 8, c, w)[2:])
         if scatter == "zy":
-            yield from self.scatter_z(c, w, scatter_z)
-            yield from self.scatter_y(r, n, c, w, scatter_y)
+            yield from self.scatter_z(c, w, scatter_z, scatter_y == 0)
+            if scatter_y == 3:
+                g = self.group()
+                for d in (2, 1, -1):
+                    self.push_y(g, (r, n, c, w), d)
+                yield g
+                self.wait(g)
+            elif scatter_y:
+                yield from self.scatter_y(r, n, c, w, scatter_y)
         else:
             yield from self.scatter_y(0, ROWS, c, w, scatter_y)
             yield from self.scatter_z(q, v, scatter_z)
-        self.finish((r, n, q, v))
+        if scatter_y == 3:
+            self.finish_rows((r, n, c, w), (r, n, q, v))
+        else:
+            self.finish((r, n, q, v))
         if gather == "yz":
-            yield from self.gather_y(r, n, c, w, gather_y)
-            yield from self.gather_z(c, w, gather_z)
+            if gather_y in (1, 2):
+                yield from self.gather_y(r, n, c, w, gather_y)
+            yield from self.gather_z(c, w, gather_z, gather_y == 0)
         else:
             yield from self.gather_z(q, v, gather_z)
             yield from self.gather_y(0, ROWS, c, w, gather_y)
@@ -321,32 +411,35 @@
 def exchange(outer_hbm, inner_hbm, momentum_hbm, full, factor, outer, inner, momentum, acc, got, sums, parts, send_sems, recv_sems, load_sems):
     ar = AllReduce(acc, got, full, send_sems, recv_sems)
     barrier = pltpu.get_barrier_semaphore()
-    for p in PEERS:
-        pl.semaphore_signal(barrier, inc=1, device_id=ar.device(**p), device_id_type=MESH)
     loads = []
     for i, (c, w, *_) in enumerate(FLOWS):
         cs = pl.ds(c, w)
         for j, (src, dst) in enumerate(((outer_hbm, outer), (inner_hbm, inner))):
             loads.append(pltpu.make_async_copy(src.at[:, cs], dst.at[:, cs], load_sems.at[2 * i + j]))
-            loads[-1].start()
-    loads.append(pltpu.make_async_copy(momentum_hbm, momentum, load_sems.at[len(loads)]))
-    loads[-1].start()
-    flows = []
-    for i, (c, w, *plan) in enumerate(FLOWS):
+    last_load = pltpu.make_async_copy(momentum_hbm, momentum, load_sems.at[len(loads)])
+    starts = list(dict.fromkeys(i for i in ORDER if i < len(FLOWS)))
+    for p in PEERS:
+        pl.semaphore_signal(barrier, inc=1, device_id=ar.device(**p), device_id_type=MESH)
+    for i in starts:
+        loads[2 * i].start()
+        loads[2 * i + 1].start()
+
+    def flow(i, c, w, *plan):
         loads[2 * i].wait()
         loads[2 * i + 1].wait()
         acc[:, pl.ds(c, w)] = outer[:, pl.ds(c, w)] - inner[:, pl.ds(c, w)].astype(jnp.float32)
-        if i == 0:
+        if i == starts[0]:
             pl.semaphore_wait(barrier, len(PEERS))
-        flows.append(ar.flow(c, w, *plan))
-        next(flows[-1])
-    flows.append(ar.clip(factor, sums, parts))
-    for i in ORDER:
+        yield from ar.flow(c, w, *plan)
+
+    flows = [flow(i, *f) for i, f in enumerate(FLOWS)] + [ar.clip(factor, sums, parts)]
+    for n, i in enumerate(ORDER):
         next(flows[i], None)
-    while flows:
-        flows = [g for g in flows if next(g, flows) is not flows]
+        if n == 2 * len(FLOWS):
+            last_load.start()
+    assert all(next(g, flows) is flows for g in flows)
     ar.drain()
-    loads[-1].wait()
+    last_load.wait()
 
 
 def all_reduce(outer_param, inner, momentum):

time: 50.1 us -> 49.3 us (0.984)
  Pallas kernels: 49.2 us -> 48.5 us
    pallas_call x1, Pallas kernels: 46.5 us -> 45.9 us  [all_reduce(): pl.pallas_call(exchange, out_shape=(array, pltpu.VMEM((8, 128), jnp.float...]
where the time goes in v3:
time: 49.3 us; the launch traced here: 49.2 us
  Pallas kernels  48.5 us (98%)
  between operations  0.64 us (1%)
    pallas_call x1, Pallas kernels, all_reduce(): pl.pallas_call(exchange, out_shape=(array, pltpu.VMEM((8, 128), jnp.float...  45.9 us
    pallas_call x1, Pallas kernels, outer_update(): pl.pallas_call(update, out_shape=[pltpu.HBM(*s) for s in shapes], in_spec...  2.69 us

profile of v3, /device:TPU:2, one launch (start us, length us, event | category | flops | bytes accessed | tf_op | source)
XLA Modules:
  0.0 49.2 jit_solution(4489748463393062647)
XLA Ops:
  0.6 45.9 %shard_map.58 = (f32[64,8192]{1,0:T(8,128)S(1)}, f32[8,128]{1,0:T(8,128)S(1)}, f32[64,8192]{1,0:T(8,128)S(1)}, bf16[64,8192]{1,0:T(8,128)(2,1)S(1)}, f32[64,8192]{1,0:T(8,128)S(1)}) custom-call(f32[64,8192]{1,0:T(8,128)} %outer_hbm.1, bf16[64,8192]{1,0:T(8,128)(2,1)} %bitcast.2, f32[64,8192]{1,0:T(8,128)} %momentum_hbm.1), custom_call_target="tpu_custom_call" | custom-call | tf_op jit(solution)/shard_map/pallas_call | solution.py:448
  46.5 2.7 %shard_map.59 = (f32[64,8192]{1,0:T(8,128)}, f32[64,8192]{1,0:T(8,128)}, bf16[64,8192]{1,0:T(8,128)(2,1)}) custom-call(f32[64,8192]{1,0:T(8,128)S(1)} %get-tuple-element.11.pseudo, f32[8,128]{1,0:T(8,128)S(1)} %get-tuple-element.12.factor, f32[64,8192]{1,0:T(8,128)S(1)} %get-tuple-element.13.outer, bf16[64,8192]{1,0:T(8,128)(2,1)S(1)} %get-tuple-element.14.inner, ...), custom_call_target="tpu_custom_call" | custom-call | tf_op jit(solution)/shard_map/pallas_call | solution.py:497

commit v4 on v3

--- a/solution.py
+++ b/solution.py
@@ -427,10 +427,22 @@
     def flow(i, c, w, *plan):
         loads[2 * i].wait()
         loads[2 * i + 1].wait()
-        acc[:, pl.ds(c, w)] = outer[:, pl.ds(c, w)] - inner[:, pl.ds(c, w)].astype(jnp.float32)
+        late = plan[0] == "yz" and plan[2] == 2
+        parts_of = [ar.quarter(d, 0, ROWS, c, w)[2:] for d in (2, 1, 3, 0)] if late else [(c, w)]
+
+        def differ(first, width):
+            cs = pl.ds(first, width)
+            acc[:, cs] = outer[:, cs] - inner[:, cs].astype(jnp.float32)
+
+        differ(*parts_of[0])
         if i == starts[0]:
             pl.semaphore_wait(barrier, len(PEERS))
-        yield from ar.flow(c, w, *plan)
+        steps = ar.flow(c, w, *plan)
+        waits = next(steps)
+        for part in parts_of[1:]:
+            differ(*part)
+        yield waits
+        yield from steps
 
     flows = [flow(i, *f) for i, f in enumerate(FLOWS)] + [ar.clip(factor, sums, parts)]
     for n, i in enumerate(ORDER):

time: 49.3 us -> 49.3 us (level)
  no operation moved by 1% of the time
where the time goes in v4:
time: 49.3 us; the launch traced here: 49.2 us
  Pallas kernels  48.5 us (98%)
  between operations  0.64 us (1%)
    pallas_call x1, Pallas kernels, all_reduce(): pl.pallas_call(exchange, out_shape=(array, pltpu.VMEM((8, 128), jnp.float...  45.9 us
    pallas_call x1, Pallas kernels, outer_update(): pl.pallas_call(update, out_shape=[pltpu.HBM(*s) for s in shapes], in_spec...  2.69 us

profile of v4, /device:TPU:2, one launch (start us, length us, event | category | flops | bytes accessed | tf_op | source)
XLA Modules:
  0.0 49.2 jit_solution(9291962066123057802)
XLA Ops:
  0.6 45.9 %shard_map.58 = (f32[64,8192]{1,0:T(8,128)S(1)}, f32[8,128]{1,0:T(8,128)S(1)}, f32[64,8192]{1,0:T(8,128)S(1)}, bf16[64,8192]{1,0:T(8,128)(2,1)S(1)}, f32[64,8192]{1,0:T(8,128)S(1)}) custom-call(f32[64,8192]{1,0:T(8,128)} %outer_hbm.1, bf16[64,8192]{1,0:T(8,128)(2,1)} %bitcast.2, f32[64,8192]{1,0:T(8,128)} %momentum_hbm.1), custom_call_target="tpu_custom_call" | custom-call | tf_op jit(solution)/shard_map/pallas_call | solution.py:460
  46.5 2.7 %shard_map.59 = (f32[64,8192]{1,0:T(8,128)}, f32[64,8192]{1,0:T(8,128)}, bf16[64,8192]{1,0:T(8,128)(2,1)}) custom-call(f32[64,8192]{1,0:T(8,128)S(1)} %get-tuple-element.11.pseudo, f32[8,128]{1,0:T(8,128)S(1)} %get-tuple-element.12.factor, f32[64,8192]{1,0:T(8,128)S(1)} %get-tuple-element.13.outer, bf16[64,8192]{1,0:T(8,128)(2,1)S(1)} %get-tuple-element.14.inner, ...), custom_call_target="tpu_custom_call" | custom-call | tf_op jit(solution)/shard_map/pallas_call | solution.py:509
